TPU v7x, 128 devices: a whole 4x4x4 slice. The times are simulated.
128 devices in a mesh: tm: 8 (over x, core), space: 16 (over z, y).
Axes of the slice: x: 4, y: 4, z: 4, core: 2. Of those that a mesh axis runs over, the one named last changes fastest.
Arguments:
- initial_voltage: float32 [4096, 128], P('space'), may hold values from -2 to 2
- initial_recovery: float32 [4096, 128], P('space'), may hold values from -0.5 to 1
- block_class: int32 [512], P('space'), may hold values from 0 to 3
- block_active: int32 [512], P('space'), may hold values 0 or 1
Outputs:
- points: float32 [16, 2, 4096, 128], P('tm', None, 'space')
Inputs may be any that keep to these rules, and one draw needn't show every extreme that they name: `block_active`: 1 marks tissue.
All inputs are finite; a program needn't handle non-finite values. No bound on the sum of `block_active` on one device may be relied on, other than what follows from the above.
Results may differ from a plain program's by a relative error of at most 0.00002.
Values sent between devices are 32-bit elements; how exact they have to be, the bound alone decides.
A program may use at most 64 MiB of HBM per device.

v0:
```python
import jax
import jax.numpy as jnp
from jax import lax
from jax.sharding import PartitionSpec as P

BR = 8
NCLASS = 4
CF = 8
CPR = 2
ITERS = 2


row_gains = (0.2, 0.35, 0.5, 0.6)
column_gains = (0.6, 0.5, 0.35, 0.2)
rate_gains = (0.06, 0.08, 0.1, 0.13)
fine_length = 0.05


def padded_2(cells, sides, width):
    for axis, dim in sides:
        count = lax.axis_size(axis)
        ends = count - 1
        head = lax.slice_in_dim(cells, 0, width, axis=dim)
        tail = lax.slice_in_dim(cells, cells.shape[dim] - width, cells.shape[dim], axis=dim)
        cells = jnp.concatenate(
            [
                lax.ppermute(tail, axis, [(i, (i + 1) % count) for i in range(ends)]),
                cells,
                lax.ppermute(head, axis, [((i + 1) % count, i) for i in range(ends)]),
            ],
            axis=dim,
        )
    return cells


def from_behind(x, axis, by):
    peers = lax.axis_size(axis)
    pairs = [(i, i + by) for i in range(peers) if 0 <= i + by < peers]
    return lax.ppermute(x, axis, pairs)


def lookup(classes, table):
    onehot = (classes[:, None] == jnp.arange(NCLASS, dtype=jnp.int32)[None, :]).astype(jnp.float32)
    return jnp.sum(onehot * jnp.array(table, dtype=jnp.float32)[None, :], axis=1)


def advance(voltage_padded, recovery, between, column_coupling, recovery_rate, active, length):
    voltage = voltage_padded[:, 1:-1]
    from_below = between[None, 1:, None] * (voltage_padded[:, 2:] - voltage)
    from_above = between[None, :-1, None] * (voltage_padded[:, :-2] - voltage)
    from_right = jnp.concatenate([voltage[..., 1:], voltage[..., -1:]], axis=-1)
    from_left = jnp.concatenate([voltage[..., :1], voltage[..., :-1]], axis=-1)
    diffusion = (
        from_below
        + from_above
        + column_coupling[None, :, None] * (from_right + from_left - 2.0 * voltage)
    )
    reaction = active[None, :, None] * (voltage - voltage**3 / 3.0 - recovery)
    new_voltage = voltage + length * (diffusion + reaction)
    new_recovery = recovery + length * recovery_rate[None, :, None] * (
        voltage + 0.7 - 0.8 * recovery
    )
    return jnp.stack([new_voltage, new_recovery], axis=1)


def local(initial_voltage, initial_recovery, block_class, block_active):
    block_info = jnp.stack([block_class, block_active])
    block_padded = padded_2(block_info, (("space", 1),), 1)
    class_rows = jnp.concatenate(
        [block_padded[0, :1], jnp.repeat(block_padded[0, 1:-1], BR), block_padded[0, -1:]]
    )
    active_rows = jnp.concatenate(
        [block_padded[1, :1], jnp.repeat(block_padded[1, 1:-1], BR), block_padded[1, -1:]]
    )
    active_pad = active_rows.astype(jnp.float32)
    coupling_pad = lookup(class_rows, row_gains)
    between = 0.5 * (coupling_pad[:-1] + coupling_pad[1:]) * active_pad[:-1] * active_pad[1:]
    active = active_pad[1:-1]
    column_coupling = lookup(class_rows[1:-1], column_gains) * active
    recovery_rate = lookup(class_rows[1:-1], rate_gains) * active
    start_state = jnp.stack([initial_voltage, initial_recovery])[None]
    coarse_length = fine_length * CF
    slices = lax.axis_size("tm")
    time_index = lax.axis_index("tm")
    leading = time_index == 0

    def advance_state(state, length):
        padded = padded_2(state[:, 0], (("space", 1),), 1)
        return advance(padded, state[:, 1], between, column_coupling, recovery_rate, active, length)

    def propagate(state):
        for repeat_index in range(CF):
            state = advance_state(state, fine_length)
        return state

    def earlier(points):
        handed = from_behind(points[-1:], "tm", 1)
        handed = jnp.where(leading, start_state, handed)
        return jnp.concatenate([handed, points[:-1]], axis=0)

    points = jnp.broadcast_to(start_state, (CPR,) + start_state.shape[1:])
    for iteration in range(ITERS):
        points = propagate(earlier(points))
        before = earlier(points)
        defect = propagate(before) - advance_state(before, coarse_length)
        incoming = start_state
        for turn_index in range(slices):
            carried = incoming
            results = []
            for position in range(CPR):
                carried = advance_state(carried, coarse_length) + defect[position : position + 1]
                results.append(carried)
            if turn_index + 1 < slices:
                passed = from_behind(carried, "tm", 1)
                incoming = jnp.where(leading, start_state, passed)
        points = jnp.concatenate(results, axis=0)
    return points


def solution(mesh):
    in_specs = (P("space", None), P("space", None), P("space"), P("space"))
    out_specs = P("tm", None, "space", None)
    return jax.shard_map(local, mesh=mesh, in_specs=in_specs, out_specs=out_specs, check_vma=False)
```

profile of v0, /device:TPU:34, one launch (start us, length us, event | category | flops | bytes accessed | tf_op | source)
XLA Modules:
  0.0 782.8 jit_solution(7053119675876336189)
XLA Ops:
  4.2 4.5 collective-permute-start.1
  23.3 5.1 collective-permute-start.5
  30.5 5.5 collective-permute-done.6
  48.4 3.9 collective-permute-start.10
  58.5 3.9 collective-permute-start.12
  98.9 3.9 collective-permute-start.20
  109.3 5.4 collective-permute-done.21
  127.0 3.9 collective-permute-start.25
  167.3 3.9 collective-permute-start.33
  208.1 5.8 collective-permute-done.40
  226.1 3.9 collective-permute-start.44
  235.9 5.8 collective-permute-done.45
  243.8 3.9 collective-permute-start.47
  263.6 5.8 collective-permute-done.50
  281.6 3.9 collective-permute-start.54
  291.4 5.8 collective-permute-done.55
  319.1 5.8 collective-permute-done.60
  337.1 3.9 collective-permute-start.64
  346.8 5.8 collective-permute-done.65
  374.6 5.8 collective-permute-done.70
  402.3 5.8 collective-permute-done.75
  410.2 4.1 collective-permute-start.77
  420.2 3.9 collective-permute-start.79
  490.7 5.8 collective-permute-done.92
  569.3 4.1 collective-permute-start.108
  589.4 5.8 collective-permute-done.111
  617.2 5.8 collective-permute-done.116
  644.9 5.8 collective-permute-done.121
  672.7 5.8 collective-permute-done.126
  700.4 5.8 collective-permute-done.131
  728.2 5.8 collective-permute-done.136
  755.9 5.8 collective-permute-done.141
  (638 shorter events, 618.5 us)
Async XLA Ops:
  0.8 12.0 %collective-permute-start = (s32[2,1]{1,0:T(2,128)S(1)}, s32[2,1]{1,0:T(2,128)S(1)}, u32[]{:S(2)}, u32[]{:S(2)}) collective-permute-start(s32[2,1]{1,0:T(2,128)S(1)} %get-tuple-element.491), channel_id=1, source_target_pairs={{0,1},{1,2},{2,3},{3,4},{4,5},{5,6},{6,7},{7,8},{8,9},{9,10},{10,1... | collective-permute-start | bytes 32 | tf_op jit(solution)/shard_map/ppermute | solution.py:27
  4.2 9.1 %collective-permute-start.1 = (s32[2,1]{1,0:T(2,128)S(1)}, s32[2,1]{1,0:T(2,128)S(1)}, u32[]{:S(2)}, u32[]{:S(2)}) collective-permute-start(s32[2,1]{1,0:T(2,128)S(1)} %get-tuple-element.492), channel_id=1, source_target_pairs={{1,0},{2,1},{3,2},{4,3},{5,4},{6,5},{7,6},{8,7},{9,8},{10,9},{11,1... | collective-permute-start | bytes 32 | tf_op jit(solution)/shard_map/ppermute | solution.py:29
  9.7 13.4 %collective-permute-start.4 = (f32[1,2,256,128]{3,2,0,1:T(8,128)S(1)}, f32[1,2,256,128]{3,2,0,1:T(8,128)S(1)}, u32[]{:S(2)}, u32[]{:S(2)}) collective-permute-start(f32[1,2,256,128]{3,2,0,1:T(8,128)S(1)} %fusion.994), channel_id=1, source_target_pairs={{0,16},{16,32},{32,48},{48,64},{64,80},{80,96},{96,112},{1,17},{17... | collective-permute-start | bytes 786440 | tf_op jit(solution)/shard_map/ppermute | solution.py:39
  17.0 92.0 %collective-permute-start.2 = (f32[1,1,128]{2,1,0:T(1,128)S(1)}, f32[1,1,128]{2,1,0:T(1,128)S(1)}, u32[]{:S(2)}, u32[]{:S(2)}) collective-permute-start(f32[1,1,128]{2,1,0:T(1,128)S(1)} %get-tuple-element.479), channel_id=1, source_target_pairs={{1,0},{2,1},{3,2},{4,3},{5,4},{6,5},{7,6},{8,7},{9,8},{10,9},{11,1... | collective-permute-start | bytes 1544 | tf_op jit(solution)/shard_map/ppermute | solution.py:29
  19.9 89.1 %collective-permute-start.3 = (f32[1,1,128]{2,1,0:T(1,128)S(1)}, f32[1,1,128]{2,1,0:T(1,128)S(1)}, u32[]{:S(2)}, u32[]{:S(2)}) collective-permute-start(f32[1,1,128]{2,1,0:T(1,128)S(1)} %get-tuple-element.480), channel_id=1, source_target_pairs={{0,1},{1,2},{2,3},{3,4},{4,5},{5,6},{6,7},{7,8},{8,9},{9,10},{10,1... | collective-permute-start | bytes 1544 | tf_op jit(solution)/shard_map/ppermute | solution.py:27
  48.4 7.6 collective-permute-start.10
  58.5 7.6 collective-permute-start.12
  98.9 7.6 collective-permute-start.20
  107.0 7.7 collective-permute-start.21
  127.0 7.6 collective-permute-start.25
  167.3 7.6 collective-permute-start.33
  206.2 7.7 collective-permute-start.40
  233.9 7.7 collective-permute-start.45
  261.7 7.7 collective-permute-start.50
  289.4 7.7 collective-permute-start.55
  317.2 7.7 collective-permute-start.60
  344.9 7.7 collective-permute-start.65
  372.7 7.7 collective-permute-start.70
  400.4 7.7 collective-permute-start.75
  420.2 7.6 collective-permute-start.79
  430.2 7.6 collective-permute-start.81
  440.3 7.6 collective-permute-start.83
  488.7 7.7 collective-permute-start.92
  498.7 7.6 collective-permute-start.94
  559.2 7.6 collective-permute-start.106
  587.5 7.7 collective-permute-start.111
  615.3 7.7 collective-permute-start.116
  643.0 7.7 collective-permute-start.121
  670.8 7.7 collective-permute-start.126
  698.5 7.7 collective-permute-start.131
  726.2 7.7 collective-permute-start.136
  754.0 7.7 collective-permute-start.141
  (121 other events, 776.1 us)
where the time goes:
time: 795 us; the launch traced here: 783 us
  starting transfers between devices  413 us (52%)
  waiting for transfers between devices  316 us (40%)
  other arithmetic  32.5 us (4%)
  local copies, waits for them, and re-layouts  17.1 us (2%)
    ppermute x64, starting transfers between devices, padded_2(): lax.ppermute(tail, axis, [(i, (i + 1) % count) for i in range(ends)])  248 us
    ppermute x64, waiting for transfers between devices, padded_2(): lax.ppermute(tail, axis, [(i, (i + 1) % count) for i in range(ends)])  219 us
    ppermute x64, starting transfers between devices, padded_2(): lax.ppermute(head, axis, [((i + 1) % count, i) for i in range(ends)])  130 us
    ppermute x18, waiting for transfers between devices, from_behind(): return lax.ppermute(x, axis, pairs)  97.6 us
    ppermute x18, starting transfers between devices, from_behind(): return lax.ppermute(x, axis, pairs)  34.6 us
  transfers between devices with their start and end apart: 146, of which 79 were waited for; matrix products, arithmetic and copies ran while one was open for 2% of the time, Pallas kernels for 0%

commit v1 on v0

v1 whole, which is shorter than its diff:
```python
import functools
import math

import jax
import jax.numpy as jnp
from jax import lax
from jax.experimental import pallas as pl
from jax.experimental.pallas import tpu as pltpu
from jax.sharding import PartitionSpec as P

MESH = pl.DeviceIdType.MESH

W = 128
BR = 8
ROWS = 256
HALF = 128
GHOST = 48
WIN = HALF + 2 * GHOST
NBLK = WIN // BR
PAD = 8
LOCAL = HALF + GHOST

row_gains = (0.2, 0.35, 0.5, 0.6)
column_gains = (0.6, 0.5, 0.35, 0.2)
rate_gains = (0.06, 0.08, 0.1, 0.13)
HF = 0.05
HG = 0.05 * 8
SF = math.sqrt(3.0 / HF)
SG = math.sqrt(3.0 / HG)
CX = SF / SG
CY = (SF / HF) / (SG / HG)


def pick(classes, table):
    out = jnp.full_like(classes, table[3])
    for i in (2, 1, 0):
        out = jnp.where(classes == float(i), table[i], out)
    return out


def span(g):
    return (GHOST - g) // 8 * 8, -(-(GHOST + HALF + g) // 8) * 8


def update(x, xu, xd, y, co):
    a0, bu, bd, cl, cr, h1, h2, h3 = co
    near = bu * xu + bd * xd
    side = cl * pltpu.roll(x, 1, 1) + cr * pltpu.roll(x, W - 1, 1)
    return (x * (a0 - x * x) - y + near) + side, h2 * y + (h1 * x + h3)


def step(src, dst, rows, co, extra=None):
    lo, hi = rows[0] + PAD, rows[1] + PAD
    sx, sy = src
    x = sx[lo:hi]
    nx, ny = update(x, sx[lo - 1 : hi - 1], sx[lo + 1 : hi + 1], sy[lo:hi], [co[q, rows[0] : rows[1]] for q in range(8)])
    if extra is not None:
        nx, ny = nx + extra[0][lo:hi], ny + extra[1][lo:hi]
    dst[0][lo:hi] = nx
    dst[1][lo:hi] = ny


def steps_of_lines(src, dst, lines, rows, co):
    for r in range(rows[0], rows[1], 8):
        c = [co[q, r : r + 8] for q in range(8)]
        lo = r + PAD
        for i in range(lines):
            sx, sy = src[0].at[i], src[1].at[i]
            nx, ny = update(sx[lo : lo + 8], sx[lo - 1 : lo + 7], sx[lo + 1 : lo + 9], sy[lo : lo + 8], c)
            dst[0][i, lo : lo + 8] = nx
            dst[1][i, lo : lo + 8] = ny


def kernel(
    u_ref, v_ref, cls_ref, act_ref, out_ref,
    uw, vw, ocls, oact, ncls, nact, tab, mask, cf, cg, fx, fy, px, py, dx, dy, lx, ly, ex, ey, rx, ry, send,
    lsem, ssem, rsem, xs, xr,
):
    t, s = lax.axis_index("tm"), lax.axis_index("space")
    chip, core = lax.div(t, 2), lax.rem(t, 2)
    to = {"space": lax.rem(s + 17 - 2 * core, 16)}
    fro = {"space": lax.rem(s + 15 + 2 * core, 16)}
    mate = {"tm": t + 1 - 2 * core}

    barrier = pltpu.get_barrier_semaphore()
    for peer in (to, fro, mate):
        pl.semaphore_signal(barrier, inc=1, device_id=peer, device_id_type=MESH)

    here = pl.multiple_of(80 * core, 8)
    there = pl.multiple_of(GHOST * (1 - core), 8)
    local = [
        pltpu.make_async_copy(u_ref.at[pl.ds(here, LOCAL)], uw.at[pl.ds(there, LOCAL)], lsem.at[0]),
        pltpu.make_async_copy(v_ref.at[pl.ds(here, LOCAL)], vw.at[pl.ds(there, LOCAL)], lsem.at[1]),
        pltpu.make_async_copy(cls_ref, ocls, lsem.at[2]),
        pltpu.make_async_copy(act_ref, oact, lsem.at[3]),
    ]
    for c in local:
        c.start()
    for buf in (fx, fy):
        for k in range(2):
            buf[k, :PAD] = jnp.zeros((PAD, W), jnp.float32)
            buf[k, PAD + WIN :] = jnp.zeros((PAD, W), jnp.float32)

    pl.semaphore_wait(barrier, 3)
    edge = pl.multiple_of((ROWS - GHOST) * (1 - core), 8)
    land = pl.multiple_of(LOCAL * core, 8)
    remote = []
    for i, (a, b) in enumerate(
        [
            (cls_ref, ncls),
            (act_ref, nact),
            (u_ref.at[pl.ds(edge, GHOST)], uw.at[pl.ds(land, GHOST)]),
            (v_ref.at[pl.ds(edge, GHOST)], vw.at[pl.ds(land, GHOST)]),
        ]
    ):
        c = pltpu.make_async_remote_copy(
            src_ref=a, dst_ref=b, send_sem=ssem.at[i], recv_sem=rsem.at[i], device_id=to, device_id_type=MESH
        )
        c.start()
        remote.append(c)
    for c in local:
        c.wait()
    for c in remote:
        c.wait()

    wi = lax.broadcasted_iota(jnp.int32, (32, 32), 0) + (16 * core - GHOST // BR)
    lane = lax.broadcasted_iota(jnp.int32, (32, 32), 1)
    own = (wi >= 0) & (wi < 32)
    hot = lane == jnp.where(wi < 0, wi + 32, jnp.where(wi >= 32, wi - 32, wi))
    gi = wi + 32 * s
    inside = (gi >= 0) & (gi < 512)
    cls = jnp.where(own, jnp.broadcast_to(ocls[...], (32, 32)), jnp.broadcast_to(ncls[...], (32, 32)))
    act = jnp.where(own, jnp.broadcast_to(oact[...], (32, 32)), jnp.broadcast_to(nact[...], (32, 32)))
    cls = jnp.where(hot, cls.astype(jnp.float32), 0.0)
    act = jnp.where(hot & inside, act.astype(jnp.float32), 0.0)
    cls = jnp.broadcast_to(jnp.sum(cls, axis=1, keepdims=True), (32, W))
    act = jnp.broadcast_to(jnp.sum(act, axis=1, keepdims=True), (32, W))
    gain = pick(cls, row_gains)
    tab[0, 8:40] = gain * act
    tab[1, 8:40] = act
    tab[2, 8:40] = gain
    tab[3, 8:40] = pick(cls, column_gains) * act
    tab[4, 8:40] = pick(cls, rate_gains) * act
    tab[1, 0:8] = jnp.zeros((8, W), jnp.float32)
    tab[2, 0:8] = jnp.zeros((8, W), jnp.float32)
    tab[5, 8:40] = 0.5 * (tab[2, 8:40] + tab[2, 7:39]) * tab[1, 8:40] * tab[1, 7:39]
    lanes = lax.broadcasted_iota(jnp.int32, (8, W), 1)
    sub = lax.broadcasted_iota(jnp.int32, (8, W), 0)
    first, last = lanes == 0, lanes == W - 1
    ends = jnp.where(first | last, 1.0, 2.0)
    for b in range(NBLK):

        def row(q, k):
            return jnp.broadcast_to(tab[q, 8 + k : 9 + k], (8, W))

        bu = jnp.where(sub == 0, row(5, b), row(0, b))
        bd = jnp.where(sub == 7, row(5, b + 1), row(0, b))
        cc, rr = row(3, b), row(4, b)
        for co, h, sc in ((cf, HF, SF), (cg, HG, SG)):
            at = slice(8 * b, 8 * b + 8)
            co[0, at] = (1.0 + h) - h * (bu + bd + cc * ends)
            co[1, at] = h * bu
            co[2, at] = h * bd
            co[3, at] = jnp.where(first, 0.0, h * cc)
            co[4, at] = jnp.where(last, 0.0, h * cc)
            co[5, at] = (h * h) * rr
            co[6, at] = 1.0 - (0.8 * h) * rr
            co[7, at] = (0.7 * h * h / sc) * rr
        if GHOST // BR <= b < (GHOST + HALF) // BR:
            mask[8 * b - GHOST : 8 * b - GHOST + 8] = row(1, b)

    def rescaled(src, dst, rows, ax, ay):
        at = slice(rows[0] + PAD, rows[1] + PAD)
        dst[0][at] = src[0][at] * ax
        dst[1][at] = src[1][at] * ay

    fine = [(fx.at[k], fy.at[k]) for k in range(2)]
    points = [(px.at[k], py.at[k]) for k in range(14)]
    shift = (dx, dy)
    chain = [(rx.at[k], ry.at[k]) for k in range(4)]
    fx[0, PAD : PAD + WIN] = uw[...] * (1.0 / SF)
    fy[0, PAD : PAD + WIN] = vw[...] * (HF / SF)
    g = 44
    for i in range(16):
        g -= 1
        step(fine[i % 2], fine[(i + 1) % 2], span(g), cf)
        if i == 7:
            rescaled(fine[0], points[0], span(g), CX, CY)
            rescaled(fine[0], chain[0], span(g), CX, CY)
    rescaled(fine[0], points[1], span(28), CX, CY)
    rescaled(fine[0], chain[1], span(28), CX, CY)
    step(points[0], shift, span(27), cg)
    lo, hi = (e + PAD for e in span(27))
    dx[lo:hi] = px[1, lo:hi] - dx[lo:hi]
    dy[lo:hi] = py[1, lo:hi] - dy[lo:hi]
    for i in range(16):
        if i < 12:
            step(points[i + 1], points[i + 2], span(27 - i), cg, shift)
        step(fine[i % 2], fine[(i + 1) % 2], span(27 - i), cf)
        if i == 7:
            rescaled(fine[0], chain[2], span(20), CX, CY)
    rescaled(fine[0], chain[3], span(12), CX, CY)

    lines = [(lx.at[k], ly.at[k]) for k in range(2)]
    for grp in (1, 2, 3):

        @pl.when(chip >= grp)
        def _():
            g = 31 - 4 * grp
            lo, hi = (e + PAD for e in span(g))
            for i in range(4):
                lx[0, i, lo:hi] = px[4 * grp - 2 + i, lo:hi] * (1.0 / CX)
                ly[0, i, lo:hi] = py[4 * grp - 2 + i, lo:hi] * (1.0 / CY)

            def two(_, c, rows):
                steps_of_lines(lines[0], lines[1], 4, rows, cf)
                steps_of_lines(lines[1], lines[0], 4, rows, cf)
                return c

            lax.fori_loop(0, 4, functools.partial(two, rows=span(g - 1)), 0)
            lo, hi = (e + PAD for e in span(g - 8))
            for i in range(4):
                lx[1, i, lo:hi] = lx[0, i, lo:hi] * CX
                ly[1, i, lo:hi] = ly[0, i, lo:hi] * CY
            steps_of_lines(lines[1], (ex, ey), 4, span(g - 9), cg)
            lax.fori_loop(0, 4, functools.partial(two, rows=span(g - 9)), 0)
            lo, hi = (e + PAD for e in span(g - 16))
            for i in range(4):
                ex[i, lo:hi] = lx[0, i, lo:hi] * CX - ex[i, lo:hi]
                ey[i, lo:hi] = ly[0, i, lo:hi] * CY - ey[i, lo:hi]
            for i in range(4):
                step(chain[(i + 3) % 4], chain[i], span(15 - 4 * grp - i), cg, (ex.at[i], ey.at[i]))

    live = mask[...] > 0.5
    mid = slice(PAD + GHOST, PAD + GHOST + HALF)
    mine = pl.ds(pl.multiple_of(HALF * core, 8), HALF)
    sends = []
    for i in range(2):
        k = 2 - 2 * core + i
        send[i, 0] = jnp.where(live, rx[k, mid] * SG, uw[GHOST : GHOST + HALF])
        send[i, 1] = jnp.where(live, ry[k, mid] * (SG / HG), vw[GHOST : GHOST + HALF])
        c = pltpu.make_async_remote_copy(
            src_ref=send.at[i], dst_ref=out_ref.at[i, :, mine], send_sem=xs.at[i], recv_sem=xr.at[i],
            device_id=mate, device_id_type=MESH,
        )
        c.start()
        sends.append(c)
    for i in range(2):
        k = 2 * core + i
        out_ref[i, 0, mine] = jnp.where(live, rx[k, mid] * SG, uw[GHOST : GHOST + HALF])
        out_ref[i, 1, mine] = jnp.where(live, ry[k, mid] * (SG / HG), vw[GHOST : GHOST + HALF])
    for c in sends:
        c.wait()


def local(initial_voltage, initial_recovery, block_class, block_active):
    f32, i32 = jnp.float32, jnp.int32
    full = PAD + WIN + PAD
    return pl.pallas_call(
        kernel,
        out_shape=jax.ShapeDtypeStruct((2, 2, ROWS, W), f32),
        in_specs=[pl.BlockSpec(memory_space=pl.ANY)] * 4,
        out_specs=pl.BlockSpec(memory_space=pltpu.VMEM),
        scratch_shapes=[
            pltpu.VMEM((WIN, W), f32),
            pltpu.VMEM((WIN, W), f32),
            *[pltpu.VMEM((1, 32), i32)] * 4,
            pltpu.VMEM((6, 48, W), f32),
            pltpu.VMEM((HALF, W), f32),
            *[pltpu.VMEM((8, WIN, W), f32)] * 2,
            *[pltpu.VMEM((2, full, W), f32)] * 2,
            *[pltpu.VMEM((14, full, W), f32)] * 2,
            *[pltpu.VMEM((full, W), f32)] * 2,
            *[pltpu.VMEM((2, 4, full, W), f32)] * 2,
            *[pltpu.VMEM((4, full, W), f32)] * 4,
            pltpu.VMEM((2, 2, HALF, W), f32),
            pltpu.SemaphoreType.DMA((4,)),
            pltpu.SemaphoreType.DMA((4,)),
            pltpu.SemaphoreType.DMA((4,)),
            pltpu.SemaphoreType.DMA((2,)),
            pltpu.SemaphoreType.DMA((2,)),
        ],
        compiler_params=pltpu.CompilerParams(
            collective_id=0, has_side_effects=True, vmem_limit_bytes=40 * 1024 * 1024
        ),
    )(initial_voltage, initial_recovery, block_class.reshape(1, 32), block_active.reshape(1, 32))


def solution(mesh):
    in_specs = (P("space", None), P("space", None), P("space"), P("space"))
    out_specs = P("tm", None, "space", None)
    return jax.shard_map(local, mesh=mesh, in_specs=in_specs, out_specs=out_specs, check_vma=False)
```

time: 795 us -> 31.1 us (0.04)
  the two profiles are of different devices: /device:TPU:34 before, /device:TPU:7 now
where the time goes in v1:
time: 31.1 us; the launch traced here: 31 us
  Pallas kernels  27.7 us (89%)
  local copies, waits for them, and re-layouts  3.27 us (11%)
    pallas_call x1, Pallas kernels, local(): pl.pallas_call(kernel, out_shape=jax.ShapeDtypeStruct((2, 2, ROWS, W), f3...  27.7 us
    unnamed x9, local copies, waits for them, and re-layouts  3.27 us

profile of v1, /device:TPU:7, one launch (start us, length us, event | category | flops | bytes accessed | tf_op | source)
XLA Modules:
  0.0 31.0 jit_solution(17996995455853276130)
XLA Ops:
  0.0 0.0 copy-start.2
  0.0 0.0 copy-start.3
  0.0 0.7 %copy-done.2 = s32[32]{0:T(128)S(1)} copy-done((s32[32]{0:T(128)S(1)}, s32[32]{0:T(128)}, u32[]{:S(2)}) %copy-start.2) | copy-done | bytes 152
  0.7 0.0 copy-done.3
  0.7 0.0 copy-start
  0.7 0.9 %copy-done = f32[256,128]{1,0:T(8,128)S(1)} copy-done((f32[256,128]{1,0:T(8,128)S(1)}, f32[256,128]{1,0:T(8,128)}, u32[]{:S(2)}) %copy-start) | copy-done | bytes 131096
  1.6 0.0 copy-start.1
  1.6 0.9 %copy-done.1 = f32[256,128]{1,0:T(8,128)S(1)} copy-done((f32[256,128]{1,0:T(8,128)S(1)}, f32[256,128]{1,0:T(8,128)}, u32[]{:S(2)}) %copy-start.1) | copy-done | bytes 131096
  2.5 27.7 %shard_map.46 = f32[2,2,256,128]{3,2,1,0:T(8,128)S(1)} custom-call(f32[256,128]{1,0:T(8,128)S(1)} %copy-done, f32[256,128]{1,0:T(8,128)S(1)} %copy-done.1, s32[1,32]{1,0:T(1,128)S(1)} %bitcast.2, s32[1,32]{1,0:T(1,128)S(1)} %bitcast.3), custom_call_target="tpu_custom_call" | custom-call | tf_op jit(solution)/shard_map/pallas_call | solution.py:259
  30.2 0.8 %copy.6 = f32[2,2,256,128]{3,2,1,0:T(8,128)} copy(f32[2,2,256,128]{3,2,1,0:T(8,128)S(1)} %shard_map.46) | data formatting | bytes 1048576
Async XLA Ops:
  0.0 0.7 %copy-start.2 = (s32[32]{0:T(128)S(1)}, s32[32]{0:T(128)}, u32[]{:S(2)}) copy-start(s32[32]{0:T(128)} %param.6) | copy-start | bytes 388
  0.0 0.7 %copy-start.3 = (s32[32]{0:T(128)S(1)}, s32[32]{0:T(128)}, u32[]{:S(2)}) copy-start(s32[32]{0:T(128)} %param.7) | copy-start | bytes 388
  0.7 0.9 %copy-start = (f32[256,128]{1,0:T(8,128)S(1)}, f32[256,128]{1,0:T(8,128)}, u32[]{:S(2)}) copy-start(f32[256,128]{1,0:T(8,128)} %u_ref.1) | copy-start | bytes 393220
  1.6 0.9 %copy-start.1 = (f32[256,128]{1,0:T(8,128)S(1)}, f32[256,128]{1,0:T(8,128)}, u32[]{:S(2)}) copy-start(f32[256,128]{1,0:T(8,128)} %v_ref.1) | copy-start | bytes 393220

commit v2 on v1

v2 whole, which is shorter than its diff:
```python
import functools
import math

import jax
import jax.numpy as jnp
from jax import lax
from jax.experimental import pallas as pl
from jax.experimental.pallas import tpu as pltpu
from jax.sharding import PartitionSpec as P

MESH = pl.DeviceIdType.MESH


W = 128
BR = 8
ROWS = 256
HALF = 128
GHOST = 48
WIN = HALF + 2 * GHOST
NBLK = WIN // BR
PAD = 8
LOCAL = HALF + GHOST
SHARE = {0: 24, 1: 48, 2: 48, 3: 24}
OFFSET = {0: (0, 120), 1: (48, 48), 2: (96, 0), 3: (24, 96)}
SIDE = 24
REACH = 40
SENDS = [(a, b) for b in (1, 2, 3) for a in (0, 3, 1, 2) if a != b]
FIRST = 4
NL = 9

row_gains = (0.2, 0.35, 0.5, 0.6)
column_gains = (0.6, 0.5, 0.35, 0.2)
rate_gains = (0.06, 0.08, 0.1, 0.13)
HF = 0.05
HG = 0.05 * 8
SF = math.sqrt(3.0 / HF)
SG = math.sqrt(3.0 / HG)
CX = SF / SG
CY = (SF / HF) / (SG / HG)


def pick(classes, table):
    out = jnp.full_like(classes, table[3])
    for i in (2, 1, 0):
        out = jnp.where(classes == float(i), table[i], out)
    return out


def span(g, side=GHOST, rows=HALF):
    return (side - g) // 8 * 8, -(-(side + rows + g) // 8) * 8


def update(x, xu, xd, y, co):
    a0, bu, bd, cl, cr, h1, h2, h3 = co
    near = bu * xu + bd * xd
    side = cl * pltpu.roll(x, 1, 1) + cr * pltpu.roll(x, W - 1, 1)
    return (x * (a0 - x * x) - y + near) + side, h2 * y + (h1 * x + h3)


def step(src, dst, rows, co, extra=None):
    lo, hi = rows[0] + PAD, rows[1] + PAD
    sx, sy = src
    x = sx[lo:hi]
    nx, ny = update(x, sx[lo - 1 : hi - 1], sx[lo + 1 : hi + 1], sy[lo:hi], [co[q, rows[0] : rows[1]] for q in range(8)])
    if extra is not None:
        nx, ny = nx + extra[0][lo:hi], ny + extra[1][lo:hi]
    dst[0][lo:hi] = nx
    dst[1][lo:hi] = ny


def line_steps(bufs, spans, co, n):
    for m in range(n):
        for i, rows in enumerate(spans):
            src, dst = bufs[m % 2], bufs[(m + 1) % 2]
            step((src[0].at[i], src[1].at[i]), (dst[0].at[i], dst[1].at[i]), rows(m), co)


def kernel(
    u_ref, v_ref, cls_ref, act_ref, out_ref,
    uw, vw, ocls, oact, ncls, nact, tab, mask, cf, cg, fx, fy, px, py, dx, dy, lx, ly, ex, ey, rx, ry, send,
    sx, sy, tx, ty, qx, qy, wf, wg, sf, sg, part, rin,
    lsem, ssem, rsem, xs, xr, ps, pr, ready,
):
    t, s = lax.axis_index("tm"), lax.axis_index("space")
    chip, core = lax.div(t, 2), lax.rem(t, 2)
    up = lax.rem(s + 17 - 2 * core, 16)
    down = lax.rem(s + 15 + 2 * core, 16)
    to, fro = {"space": up}, {"space": down}
    sends_edge = s != 15 * (1 - core)
    takes_edge = s != 15 * core
    mate = {"tm": t + 1 - 2 * core}

    barrier = pltpu.get_barrier_semaphore()
    pl.semaphore_signal(barrier, inc=1, device_id=mate, device_id_type=MESH)

    @pl.when(takes_edge)
    def _():
        pl.semaphore_signal(barrier, inc=1, device_id=fro, device_id_type=MESH)

    for a, b in ((0, 1), (2, 1), (3, 1), (1, 2), (3, 2)):

        @pl.when(chip == a)
        def _(b=b):
            pl.semaphore_signal(barrier, inc=1, device_id={"tm": 2 * b + core}, device_id_type=MESH)

    here = pl.multiple_of(80 * core, 8)
    there = pl.multiple_of(GHOST * (1 - core), 8)
    local = [
        pltpu.make_async_copy(u_ref.at[pl.ds(here, LOCAL)], uw.at[pl.ds(there, LOCAL)], lsem.at[0]),
        pltpu.make_async_copy(v_ref.at[pl.ds(here, LOCAL)], vw.at[pl.ds(there, LOCAL)], lsem.at[1]),
        pltpu.make_async_copy(cls_ref, ocls, lsem.at[2]),
        pltpu.make_async_copy(act_ref, oact, lsem.at[3]),
    ]
    for c in local:
        c.start()
    for buf in (fx, fy):
        for k in range(2):
            buf[k, :PAD] = jnp.zeros((PAD, W), jnp.float32)
            buf[k, PAD + WIN :] = jnp.zeros((PAD, W), jnp.float32)

    pl.semaphore_wait(barrier, 1 + sends_edge.astype(jnp.int32) + jnp.where(chip == 1, 3, jnp.where(chip == 2, 2, 0)))
    edge = pl.multiple_of((ROWS - GHOST) * (1 - core), 8)
    land = pl.multiple_of(LOCAL * core, 8)
    edges = [
        (cls_ref, ncls),
        (act_ref, nact),
        (u_ref.at[pl.ds(edge, GHOST)], uw.at[pl.ds(land, GHOST)]),
        (v_ref.at[pl.ds(edge, GHOST)], vw.at[pl.ds(land, GHOST)]),
    ]
    remote = [
        pltpu.make_async_remote_copy(
            src_ref=a, dst_ref=b, send_sem=ssem.at[i], recv_sem=rsem.at[i], device_id=to, device_id_type=MESH
        )
        for i, (a, b) in enumerate(edges)
    ]

    @pl.when(sends_edge)
    def _():
        for c in remote:
            c.start()

    @pl.when(chip == 1)
    def _():
        for a in (0, 3):
            pl.semaphore_signal(ready, inc=1, device_id={"tm": 2 * a + core}, device_id_type=MESH)

    for c in local:
        c.wait()

    def tables(edges_here):
        wi = lax.broadcasted_iota(jnp.int32, (32, 32), 0) + (16 * core - GHOST // BR)
        lane = lax.broadcasted_iota(jnp.int32, (32, 32), 1)
        own = (wi >= 0) & (wi < 32)
        hot = lane == jnp.where(wi < 0, wi + 32, jnp.where(wi >= 32, wi - 32, wi))
        gi = wi + 32 * s
        inside = (gi >= 0) & (gi < 512)
        cls = jnp.broadcast_to(ocls[...], (32, 32))
        act = jnp.broadcast_to(oact[...], (32, 32))
        if edges_here:
            cls = jnp.where(own, cls, jnp.broadcast_to(ncls[...], (32, 32)))
            act = jnp.where(own, act, jnp.broadcast_to(nact[...], (32, 32)))
        cls = jnp.where(hot, cls.astype(jnp.float32), 0.0)
        act = jnp.where(hot & inside, act.astype(jnp.float32), 0.0)
        cls = jnp.broadcast_to(jnp.sum(cls, axis=1, keepdims=True), (32, W))
        act = jnp.broadcast_to(jnp.sum(act, axis=1, keepdims=True), (32, W))
        gain = pick(cls, row_gains)
        tab[0, 8:40] = gain * act
        tab[1, 8:40] = act
        tab[2, 8:40] = gain
        tab[3, 8:40] = pick(cls, column_gains) * act
        tab[4, 8:40] = pick(cls, rate_gains) * act
        tab[1, 0:8] = jnp.zeros((8, W), jnp.float32)
        tab[2, 0:8] = jnp.zeros((8, W), jnp.float32)
        tab[5, 8:40] = 0.5 * (tab[2, 8:40] + tab[2, 7:39]) * tab[1, 8:40] * tab[1, 7:39]
        lanes = lax.broadcasted_iota(jnp.int32, (8, W), 1)
        sub = lax.broadcasted_iota(jnp.int32, (8, W), 0)
        first, last = lanes == 0, lanes == W - 1
        ends = jnp.where(first | last, 1.0, 2.0)
        for b in range(NBLK):

            def row(q, k):
                return jnp.broadcast_to(tab[q, 8 + k : 9 + k], (8, W))

            bu = jnp.where(sub == 0, row(5, b), row(0, b))
            bd = jnp.where(sub == 7, row(5, b + 1), row(0, b))
            cc, rr = row(3, b), row(4, b)
            for co, h, sc in ((cf, HF, SF), (cg, HG, SG)):
                at = slice(8 * b, 8 * b + 8)
                co[0, at] = (1.0 + h) - h * (bu + bd + cc * ends)
                co[1, at] = h * bu
                co[2, at] = h * bd
                co[3, at] = jnp.where(first, 0.0, h * cc)
                co[4, at] = jnp.where(last, 0.0, h * cc)
                co[5, at] = (h * h) * rr
                co[6, at] = 1.0 - (0.8 * h) * rr
                co[7, at] = (0.7 * h * h / sc) * rr
            if GHOST // BR <= b < (GHOST + HALF) // BR:
                mask[8 * b - GHOST : 8 * b - GHOST + 8] = row(1, b)

    def rescaled(src, dst, rows, ax, ay):
        at = slice(rows[0] + PAD, rows[1] + PAD)
        dst[0][at] = src[0][at] * ax
        dst[1][at] = src[1][at] * ay

    fine = [(fx.at[k], fy.at[k]) for k in range(2)]
    points = [(px.at[k], py.at[k]) for k in range(14)]
    shift = (dx, dy)
    chain = [(rx.at[k], ry.at[k]) for k in range(4)]
    def prepare(span, ghost, last, co, cg):
        for i in range(16):
            step(fine[i % 2], fine[(i + 1) % 2], span(ghost - 1 - i), co)
            if i == 7:
                rescaled(fine[0], points[0], span(ghost - 8), CX, CY)
        rescaled(fine[0], points[1], span(ghost - 16), CX, CY)
        step(points[0], shift, span(ghost - 17), cg)
        lo, hi = (e + PAD for e in span(ghost - 17))
        dx[lo:hi] = px[1, lo:hi] - dx[lo:hi]
        dy[lo:hi] = py[1, lo:hi] - dy[lo:hi]
        go_on(span, ghost, 3, last, cg)

    def go_on(span, ghost, first, last, cg):
        for j in range(first, last + 1):
            step(points[j - 2], points[j - 1], span(ghost - 14 - j), cg, shift)

    def sending(a, b):
        at = pl.multiple_of(OFFSET[a][0] + (OFFSET[a][1] - OFFSET[a][0]) * core, 8)
        return pltpu.make_async_remote_copy(
            src_ref=part.at[b - 1, :, pl.ds(0, SHARE[a])], dst_ref=rin.at[:, pl.ds(at, SHARE[a])],
            send_sem=ps.at[b - 1], recv_sem=pr.at[a], device_id={"tm": 2 * b + core}, device_id_type=MESH,
        )

    def share(chips, at, sf, sg):
        n = SHARE[chips[0]]
        long = n + 2 * SIDE
        for i in range(NL):
            sx[0, i, PAD : PAD + long] = px[i + 1, pl.ds(at, long)] * (1.0 / CX)
            sy[0, i, PAD : PAD + long] = py[i + 1, pl.ds(at, long)] * (1.0 / CY)
        rows = functools.partial(span, side=SIDE, rows=n)
        lines = [(sx.at[k], sy.at[k]) for k in range(2)]
        line_steps(lines, [lambda m, i=i: rows(23 - i - m) for i in range(NL)], sf, 8)
        for i in range(1, NL):
            rescaled((sx.at[0, i], sy.at[0, i]), (sx.at[1, i], sy.at[1, i]), rows(16 - i), CX, CY)
            step((sx.at[1, i], sy.at[1, i]), (qx.at[i], qy.at[i]), rows(8 - i), sg)
        line_steps(lines, [lambda m, i=i: rows(15 - i - m) for i in range(NL)], sf, 8)
        rescaled((sx.at[0, 0], sy.at[0, 0]), (tx.at[0], ty.at[0]), rows(8), CX, CY)
        for i in range(1, NL):
            lo, hi = (e + PAD for e in rows(8 - i))
            qx[i, lo:hi] = sx[0, i, lo:hi] * CX - qx[i, lo:hi]
            qy[i, lo:hi] = sy[0, i, lo:hi] * CY - qy[i, lo:hi]
        mid = slice(PAD + SIDE, PAD + SIDE + n)
        for i in range(NL):
            if i:
                step((tx.at[i - 1], ty.at[i - 1]), (tx.at[i], ty.at[i]), rows(8 - i), sg, (qx.at[i], qy.at[i]))
            if i % 4 == 0:
                b = i // 4 + 1
                part[b - 1, 0, 0:n] = tx[i, mid]
                part[b - 1, 1, 0:n] = ty[i, mid]
                if i == 0 and 0 in chips:
                    pl.semaphore_wait(ready, 1)
                for a in chips:

                    @pl.when(chip == a)
                    def _(a=a, b=b):
                        if a != b:
                            sending(a, b).start()
                        else:
                            own = pl.multiple_of(OFFSET[a][0] + (OFFSET[a][1] - OFFSET[a][0]) * core, 8)
                            rin[:, pl.ds(own, n)] = part[b - 1, :, 0:n]

    def offset(a, b):
        x = jnp.where(chip == a, OFFSET[a][0], OFFSET[b][0])
        y = jnp.where(chip == a, OFFSET[a][1], OFFSET[b][1])
        return GHOST - 8 + jnp.where(core == 0, x, y)

    @pl.when((chip == 1) | (chip == 2))
    def _():
        tables(False)
        n = SHARE[1]
        long = n + 2 * REACH
        base = pl.multiple_of(offset(1, 2) - REACH, 8)
        for q in range(8):
            wf[q] = cf[q, pl.ds(base, long)]
            wg[q] = cg[q, pl.ds(base, long)]
            sf[q] = cf[q, pl.ds(pl.multiple_of(base + REACH - SIDE, 8), n + 2 * SIDE)]
            sg[q] = cg[q, pl.ds(pl.multiple_of(base + REACH - SIDE, 8), n + 2 * SIDE)]
        fx[0, PAD : PAD + long] = uw[pl.ds(base, long)] * (1.0 / SF)
        fy[0, PAD : PAD + long] = vw[pl.ds(base, long)] * (HF / SF)
        prepare(functools.partial(span, side=REACH, rows=n), REACH, 10, wf, wg)
        share((1, 2), PAD + REACH - SIDE, sf, sg)

    @pl.when(takes_edge)
    def _():
        for c in remote:
            c.wait_recv()

    @pl.when(jnp.logical_not(takes_edge))
    def _():
        uw[pl.ds(land, GHOST)] = jnp.zeros((GHOST, W), jnp.float32)
        vw[pl.ds(land, GHOST)] = jnp.zeros((GHOST, W), jnp.float32)
        ncls[...] = jnp.zeros((1, 32), jnp.int32)
        nact[...] = jnp.zeros((1, 32), jnp.int32)

    tables(True)
    fx[0, PAD : PAD + WIN] = uw[...] * (1.0 / SF)
    fy[0, PAD : PAD + WIN] = vw[...] * (HF / SF)
    prepare(span, GHOST, 6, cf, cg)

    @pl.when(chip != 1)
    def _():
        go_on(span, GHOST, 7, 10, cg)

    @pl.when((chip == 0) | (chip == 3))
    def _():
        n = SHARE[0]
        base = pl.multiple_of(offset(0, 3) - SIDE, 8)
        for q in range(8):
            sf[q, 0 : n + 2 * SIDE] = cf[q, pl.ds(base, n + 2 * SIDE)]
            sg[q, 0 : n + 2 * SIDE] = cg[q, pl.ds(base, n + 2 * SIDE)]
        share((0, 3), pl.multiple_of(base + PAD, 8), sf, sg)

    @pl.when(chip == 0)
    def _():
        for i in range(16):
            step(fine[i % 2], fine[(i + 1) % 2], span(15 - i), cf)
            if i == 7:
                rescaled(fine[0], chain[2], span(0), CX, CY)
        rescaled(fine[0], chain[3], span(0), CX, CY)
        for k in range(2):
            rescaled(points[k], chain[k], span(0), 1.0, 1.0)

    @pl.when(chip == 3)
    def _():
        go_on(span, GHOST, 11, 14, cg)

    @pl.when(chip > 0)
    def _():
        lines = [(lx.at[k], ly.at[k]) for k in range(2)]
        lo, hi = (e + PAD for e in span(19))
        for i in range(4):
            k = 4 * chip - 2 + i
            lx[0, i, lo:hi] = px[k, lo:hi] * (1.0 / CX)
            ly[0, i, lo:hi] = py[k, lo:hi] * (1.0 / CY)
        line_steps(lines, [lambda m, i=i: span(18 - i - m) for i in range(4)], cf, 8)
        for i in range(4):
            rescaled((lx.at[0, i], ly.at[0, i]), (lx.at[1, i], ly.at[1, i]), span(11 - i), CX, CY)
            step((lx.at[1, i], ly.at[1, i]), (ex.at[i], ey.at[i]), span(3 - i), cg)
        line_steps(lines, [lambda m, i=i: span(10 - i - m) for i in range(4)], cf, 8)
        for i in range(4):
            lo, hi = (e + PAD for e in span(3 - i))
            ex[i, lo:hi] = lx[0, i, lo:hi] * CX - ex[i, lo:hi]
            ey[i, lo:hi] = ly[0, i, lo:hi] * CY - ey[i, lo:hi]
        for a in range(4):

            @pl.when(chip != a)
            def _(a=a):
                sending(a, 1).wait_recv()

        at = slice(PAD + GHOST - 8, PAD + GHOST + HALF + 8)
        rx[3, at] = rin[0]
        ry[3, at] = rin[1]
        for i in range(4):
            step(chain[(i + 3) % 4], chain[i], span(3 - i), cg, (ex.at[i], ey.at[i]))

    live = mask[...] > 0.5
    mid = slice(PAD + GHOST, PAD + GHOST + HALF)
    mine = pl.ds(pl.multiple_of(HALF * core, 8), HALF)
    sends = []
    for i in range(2):
        k = 2 - 2 * core + i
        send[i, 0] = jnp.where(live, rx[k, mid] * SG, uw[GHOST : GHOST + HALF])
        send[i, 1] = jnp.where(live, ry[k, mid] * (SG / HG), vw[GHOST : GHOST + HALF])
        c = pltpu.make_async_remote_copy(
            src_ref=send.at[i], dst_ref=out_ref.at[i, :, mine], send_sem=xs.at[i], recv_sem=xr.at[i],
            device_id=mate, device_id_type=MESH,
        )
        c.start()
        sends.append(c)
    for i in range(2):
        k = 2 * core + i
        out_ref[i, 0, mine] = jnp.where(live, rx[k, mid] * SG, uw[GHOST : GHOST + HALF])
        out_ref[i, 1, mine] = jnp.where(live, ry[k, mid] * (SG / HG), vw[GHOST : GHOST + HALF])
    for c in sends:
        c.wait()
    for a, b in SENDS:

        @pl.when(chip == a)
        def _(a=a, b=b):
            sending(a, b).wait_send()

    @pl.when(sends_edge)
    def _():
        for c in remote:
            c.wait_send()


def local(initial_voltage, initial_recovery, block_class, block_active):
    f32, i32 = jnp.float32, jnp.int32
    given = (initial_voltage, initial_recovery, block_class.reshape(1, 32), block_active.reshape(1, 32))
    given = [pltpu.with_memory_space_constraint(x, pltpu.HBM) for x in given]
    full = PAD + WIN + PAD
    share = PAD + SHARE[1] + 2 * SIDE + PAD
    return pl.pallas_call(
        kernel,
        out_shape=jax.ShapeDtypeStruct((2, 2, ROWS, W), f32),
        in_specs=[pl.BlockSpec(memory_space=pltpu.HBM)] * 4,
        out_specs=pl.BlockSpec(memory_space=pltpu.VMEM),
        scratch_shapes=[
            pltpu.VMEM((WIN, W), f32),
            pltpu.VMEM((WIN, W), f32),
            *[pltpu.VMEM((1, 32), i32)] * 4,
            pltpu.VMEM((6, 48, W), f32),
            pltpu.VMEM((HALF, W), f32),
            *[pltpu.VMEM((8, WIN, W), f32)] * 2,
            *[pltpu.VMEM((2, full, W), f32)] * 2,
            *[pltpu.VMEM((14, full, W), f32)] * 2,
            *[pltpu.VMEM((full, W), f32)] * 2,
            *[pltpu.VMEM((2, 4, full, W), f32)] * 2,
            *[pltpu.VMEM((4, full, W), f32)] * 4,
            pltpu.VMEM((2, 2, HALF, W), f32),
            *[pltpu.VMEM((2, NL, share, W), f32)] * 2,
            *[pltpu.VMEM((NL, share, W), f32)] * 4,
            *[pltpu.VMEM((8, SHARE[1] + 2 * REACH, W), f32)] * 2,
            *[pltpu.VMEM((8, SHARE[1] + 2 * SIDE, W), f32)] * 2,
            pltpu.VMEM((3, 2, SHARE[1], W), f32),
            pltpu.VMEM((2, 144, W), f32),
            pltpu.SemaphoreType.DMA((4,)),
            pltpu.SemaphoreType.DMA((4,)),
            pltpu.SemaphoreType.DMA((4,)),
            pltpu.SemaphoreType.DMA((2,)),
            pltpu.SemaphoreType.DMA((2,)),
            pltpu.SemaphoreType.DMA((3,)),
            pltpu.SemaphoreType.DMA((4,)),
            pltpu.SemaphoreType.REGULAR,
        ],
        compiler_params=pltpu.CompilerParams(
            collective_id=0, has_side_effects=True, vmem_limit_bytes=40 * 1024 * 1024
        ),
    )(*given)


def solution(mesh):
    in_specs = (P("space", None), P("space", None), P("space"), P("space"))
    out_specs = P("tm", None, "space", None)
    return jax.shard_map(local, mesh=mesh, in_specs=in_specs, out_specs=out_specs, check_vma=False)
```

time: 31.1 us -> 20.3 us (0.65)
  the two profiles are of different devices: /device:TPU:7 before, /device:TPU:71 now
where the time goes in v2:
time: 20.3 us; the launch traced here: 20.2 us
  Pallas kernels  19.4 us (96%)
  local copies, waits for them, and re-layouts  0.8 us (4%)
    pallas_call x1, Pallas kernels, local(): pl.pallas_call(kernel, out_shape=jax.ShapeDtypeStruct((2, 2, ROWS, W), f3...  19.4 us
    unnamed x1, local copies, waits for them, and re-layouts  0.8 us

profile of v2, /device:TPU:71, one launch (start us, length us, event | category | flops | bytes accessed | tf_op | source)
XLA Modules:
  0.0 20.2 jit_solution(12631431783718376986)
XLA Ops:
  0.0 19.4 %shard_map.46 = f32[2,2,256,128]{3,2,1,0:T(8,128)S(1)} custom-call(f32[256,128]{1,0:T(8,128)} %u_ref.1, f32[256,128]{1,0:T(8,128)} %v_ref.1, s32[1,32]{1,0:T(1,128)} %bitcast.2, s32[1,32]{1,0:T(1,128)} %bitcast.3), custom_call_target="tpu_custom_call" | custom-call | tf_op jit(solution)/shard_map/pallas_call | solution.py:402
  19.4 0.8 %copy.6 = f32[2,2,256,128]{3,2,1,0:T(8,128)} copy(f32[2,2,256,128]{3,2,1,0:T(8,128)S(1)} %shard_map.46) | data formatting | bytes 1048576

commit v3 on v2

--- a/solution.py
+++ b/solution.py
@@ -20,11 +20,10 @@
 NBLK = WIN // BR
 PAD = 8
 LOCAL = HALF + GHOST
-SHARE = {0: 24, 1: 48, 2: 48, 3: 24}
-OFFSET = {0: (0, 120), 1: (48, 48), 2: (96, 0), 3: (24, 96)}
+SHARE = 48
 SIDE = 24
 REACH = 40
-SENDS = [(a, b) for b in (1, 2, 3) for a in (0, 3, 1, 2) if a != b]
+SENDS = [(a, b) for b in (1, 2, 3) for a in (0, 1, 2) if a != b]
 FIRST = 4
 NL = 9
 
@@ -57,22 +56,27 @@
     return (x * (a0 - x * x) - y + near) + side, h2 * y + (h1 * x + h3)
 
 
-def step(src, dst, rows, co, extra=None):
-    lo, hi = rows[0] + PAD, rows[1] + PAD
+def step(src, dst, rows, co, extra=None, chunk=32):
     sx, sy = src
-    x = sx[lo:hi]
-    nx, ny = update(x, sx[lo - 1 : hi - 1], sx[lo + 1 : hi + 1], sy[lo:hi], [co[q, rows[0] : rows[1]] for q in range(8)])
-    if extra is not None:
-        nx, ny = nx + extra[0][lo:hi], ny + extra[1][lo:hi]
-    dst[0][lo:hi] = nx
-    dst[1][lo:hi] = ny
-
-
-def line_steps(bufs, spans, co, n):
-    for m in range(n):
-        for i, rows in enumerate(spans):
-            src, dst = bufs[m % 2], bufs[(m + 1) % 2]
-            step((src[0].at[i], src[1].at[i]), (dst[0].at[i], dst[1].at[i]), rows(m), co)
+    for r in range(rows[0], rows[1], chunk):
+        end = min(r + chunk, rows[1])
+        lo, hi = r + PAD, end + PAD
+        c = [co[q, r:end] for q in range(8)]
+        nx, ny = update(sx[lo:hi], sx[lo - 1 : hi - 1], sx[lo + 1 : hi + 1], sy[lo:hi], c)
+        if extra is not None:
+            nx, ny = nx + extra[0][lo:hi], ny + extra[1][lo:hi]
+        dst[0][lo:hi] = nx
+        dst[1][lo:hi] = ny
+
+
+def line_steps(jobs, co, chunk=16):
+    first = min((rows[0] for _, _, rows in jobs), default=0)
+    last = max((rows[1] for _, _, rows in jobs), default=0)
+    for r in range(first, last, chunk):
+        for src, dst, (lo, hi) in jobs:
+            part = max(lo, r), min(hi, r + chunk)
+            if part[0] < part[1]:
+                step(src, dst, part, co, chunk=chunk)
 
 
 def kernel(
@@ -117,35 +121,6 @@
         for k in range(2):
             buf[k, :PAD] = jnp.zeros((PAD, W), jnp.float32)
             buf[k, PAD + WIN :] = jnp.zeros((PAD, W), jnp.float32)
-
-    pl.semaphore_wait(barrier, 1 + sends_edge.astype(jnp.int32) + jnp.where(chip == 1, 3, jnp.where(chip == 2, 2, 0)))
-    edge = pl.multiple_of((ROWS - GHOST) * (1 - core), 8)
-    land = pl.multiple_of(LOCAL * core, 8)
-    edges = [
-        (cls_ref, ncls),
-        (act_ref, nact),
-        (u_ref.at[pl.ds(edge, GHOST)], uw.at[pl.ds(land, GHOST)]),
-        (v_ref.at[pl.ds(edge, GHOST)], vw.at[pl.ds(land, GHOST)]),
-    ]
-    remote = [
-        pltpu.make_async_remote_copy(
-            src_ref=a, dst_ref=b, send_sem=ssem.at[i], recv_sem=rsem.at[i], device_id=to, device_id_type=MESH
-        )
-        for i, (a, b) in enumerate(edges)
-    ]
-
-    @pl.when(sends_edge)
-    def _():
-        for c in remote:
-            c.start()
-
-    @pl.when(chip == 1)
-    def _():
-        for a in (0, 3):
-            pl.semaphore_signal(ready, inc=1, device_id={"tm": 2 * a + core}, device_id_type=MESH)
-
-    for c in local:
-        c.wait()
 
     def tables(edges_here):
         wi = lax.broadcasted_iota(jnp.int32, (32, 32), 0) + (16 * core - GHOST // BR)
@@ -222,134 +197,201 @@
         for j in range(first, last + 1):
             step(points[j - 2], points[j - 1], span(ghost - 14 - j), cg, shift)
 
+    def begins(a):
+        return pl.multiple_of(SHARE * (a + (2 - 2 * a) * core), 8)
+
     def sending(a, b):
-        at = pl.multiple_of(OFFSET[a][0] + (OFFSET[a][1] - OFFSET[a][0]) * core, 8)
         return pltpu.make_async_remote_copy(
-            src_ref=part.at[b - 1, :, pl.ds(0, SHARE[a])], dst_ref=rin.at[:, pl.ds(at, SHARE[a])],
-            send_sem=ps.at[b - 1], recv_sem=pr.at[a], device_id={"tm": 2 * b + core}, device_id_type=MESH,
+            src_ref=part.at[b - 1], dst_ref=rin.at[:, pl.ds(begins(a), SHARE)], send_sem=ps.at[b - 1], recv_sem=pr.at[a],
+            device_id={"tm": 2 * b + core}, device_id_type=MESH,
         )
 
-    def share(chips, at, sf, sg):
-        n = SHARE[chips[0]]
-        long = n + 2 * SIDE
-        for i in range(NL):
-            sx[0, i, PAD : PAD + long] = px[i + 1, pl.ds(at, long)] * (1.0 / CX)
-            sy[0, i, PAD : PAD + long] = py[i + 1, pl.ds(at, long)] * (1.0 / CY)
-        rows = functools.partial(span, side=SIDE, rows=n)
-        lines = [(sx.at[k], sy.at[k]) for k in range(2)]
-        line_steps(lines, [lambda m, i=i: rows(23 - i - m) for i in range(NL)], sf, 8)
-        for i in range(1, NL):
-            rescaled((sx.at[0, i], sy.at[0, i]), (sx.at[1, i], sy.at[1, i]), rows(16 - i), CX, CY)
-            step((sx.at[1, i], sy.at[1, i]), (qx.at[i], qy.at[i]), rows(8 - i), sg)
-        line_steps(lines, [lambda m, i=i: rows(15 - i - m) for i in range(NL)], sf, 8)
-        rescaled((sx.at[0, 0], sy.at[0, 0]), (tx.at[0], ty.at[0]), rows(8), CX, CY)
-        for i in range(1, NL):
-            lo, hi = (e + PAD for e in rows(8 - i))
-            qx[i, lo:hi] = sx[0, i, lo:hi] * CX - qx[i, lo:hi]
-            qy[i, lo:hi] = sy[0, i, lo:hi] * CY - qy[i, lo:hi]
-        mid = slice(PAD + SIDE, PAD + SIDE + n)
-        for i in range(NL):
-            if i:
-                step((tx.at[i - 1], ty.at[i - 1]), (tx.at[i], ty.at[i]), rows(8 - i), sg, (qx.at[i], qy.at[i]))
-            if i % 4 == 0:
+    wide = functools.partial(span, side=REACH, rows=SHARE)
+
+    def share_begins():
+        base = pl.multiple_of(GHOST - 8 - REACH + begins(chip), 8)
+        long = SHARE + 2 * REACH
+        inner = pl.multiple_of(base + REACH - SIDE, 8)
+        for q in range(8):
+            wf[q] = cf[q, pl.ds(base, long)]
+            wg[q] = cg[q, pl.ds(base, long)]
+            sf[q] = cf[q, pl.ds(inner, SHARE + 2 * SIDE)]
+            sg[q] = cg[q, pl.ds(inner, SHARE + 2 * SIDE)]
+        fx[0, PAD : PAD + long] = uw[pl.ds(base, long)] * (1.0 / SF)
+        fy[0, PAD : PAD + long] = vw[pl.ds(base, long)] * (HF / SF)
+        prepare(wide, REACH, 2, wf, wg)
+
+    def share():
+        at = slice(PAD + REACH - SIDE, PAD + REACH + SHARE + SIDE)
+        own = slice(PAD, PAD + SHARE + 2 * SIDE)
+        mid = slice(PAD + SIDE, PAD + SIDE + SHARE)
+        rows = functools.partial(span, side=SIDE, rows=SHARE)
+
+        def line(m, i):
+            return sx.at[m % 2, i], sy.at[m % 2, i]
+
+        def link(i):
+            return tx.at[i], ty.at[i]
+
+        for tick in range(16 + 2 * NL):
+            if 0 <= tick < NL - 1:
+                go_on(wide, REACH, tick + 3, tick + 3, wg)
+            if 0 <= tick < NL:
+                sx[0, tick, own] = px[tick + 1, at] * (1.0 / CX)
+                sy[0, tick, own] = py[tick + 1, at] * (1.0 / CY)
+            i = tick - 16
+            if 0 <= i < NL:
+                if i == 0:
+                    rescaled(line(0, 0), link(0), rows(8), CX, CY)
+                else:
+                    lo, hi = (e + PAD for e in rows(8 - i))
+                    qx[i, lo:hi] = sx[0, i, lo:hi] * CX - qx[i, lo:hi]
+                    qy[i, lo:hi] = sy[0, i, lo:hi] * CY - qy[i, lo:hi]
+                    step(link(i - 1), link(i), rows(8 - i), sg, (qx.at[i], qy.at[i]))
+                if i % 4 == 0:
+                    b = i // 4
+                    part[b, 0] = tx[i, mid]
+                    part[b, 1] = ty[i, mid]
+            line_steps(
+                [
+                    (line(m, i), line(m + 1, i), rows(23 - i - m))
+                    for i in range(NL)
+                    for m in (tick - i,)
+                    if 0 <= m < 16
+                ],
+                sf,
+            )
+            i = tick - 7
+            if 1 <= i < NL:
+                rescaled(line(0, i), line(1, i), rows(16 - i), CX, CY)
+                step(line(1, i), (qx.at[i], qy.at[i]), rows(8 - i), sg)
+
+            i = tick - 16
+            if i in (0, 4, 8):
+
+                @pl.when(chip == 0)
+                def _():
+                    if i == 0:
+                        pl.semaphore_wait(ready, 1)
+
                 b = i // 4 + 1
-                part[b - 1, 0, 0:n] = tx[i, mid]
-                part[b - 1, 1, 0:n] = ty[i, mid]
-                if i == 0 and 0 in chips:
-                    pl.semaphore_wait(ready, 1)
-                for a in chips:
+                for a in range(3):
 
                     @pl.when(chip == a)
                     def _(a=a, b=b):
                         if a != b:
                             sending(a, b).start()
                         else:
-                            own = pl.multiple_of(OFFSET[a][0] + (OFFSET[a][1] - OFFSET[a][0]) * core, 8)
-                            rin[:, pl.ds(own, n)] = part[b - 1, :, 0:n]
-
-    def offset(a, b):
-        x = jnp.where(chip == a, OFFSET[a][0], OFFSET[b][0])
-        y = jnp.where(chip == a, OFFSET[a][1], OFFSET[b][1])
-        return GHOST - 8 + jnp.where(core == 0, x, y)
+                            rin[:, pl.ds(begins(a), SHARE)] = part[b - 1]
 
     @pl.when((chip == 1) | (chip == 2))
     def _():
+        for c in local:
+            c.wait()
         tables(False)
-        n = SHARE[1]
-        long = n + 2 * REACH
-        base = pl.multiple_of(offset(1, 2) - REACH, 8)
-        for q in range(8):
-            wf[q] = cf[q, pl.ds(base, long)]
-            wg[q] = cg[q, pl.ds(base, long)]
-            sf[q] = cf[q, pl.ds(pl.multiple_of(base + REACH - SIDE, 8), n + 2 * SIDE)]
-            sg[q] = cg[q, pl.ds(pl.multiple_of(base + REACH - SIDE, 8), n + 2 * SIDE)]
-        fx[0, PAD : PAD + long] = uw[pl.ds(base, long)] * (1.0 / SF)
-        fy[0, PAD : PAD + long] = vw[pl.ds(base, long)] * (HF / SF)
-        prepare(functools.partial(span, side=REACH, rows=n), REACH, 10, wf, wg)
-        share((1, 2), PAD + REACH - SIDE, sf, sg)
-
-    @pl.when(takes_edge)
+        share_begins()
+
+    pl.semaphore_wait(barrier, 1 + sends_edge.astype(jnp.int32) + jnp.where(chip == 1, 3, jnp.where(chip == 2, 2, 0)))
+    edge = pl.multiple_of((ROWS - GHOST) * (1 - core), 8)
+    land = pl.multiple_of(LOCAL * core, 8)
+    edges = [
+        (u_ref.at[pl.ds(edge, GHOST)], uw.at[pl.ds(land, GHOST)]),
+        (v_ref.at[pl.ds(edge, GHOST)], vw.at[pl.ds(land, GHOST)]),
+        (cls_ref, ncls),
+        (act_ref, nact),
+    ]
+    remote = [
+        pltpu.make_async_remote_copy(
+            src_ref=a, dst_ref=b, send_sem=ssem.at[i], recv_sem=rsem.at[i], device_id=to, device_id_type=MESH
+        )
+        for i, (a, b) in enumerate(edges)
+    ]
+
+    @pl.when(sends_edge)
     def _():
         for c in remote:
-            c.wait_recv()
-
-    @pl.when(jnp.logical_not(takes_edge))
-    def _():
-        uw[pl.ds(land, GHOST)] = jnp.zeros((GHOST, W), jnp.float32)
-        vw[pl.ds(land, GHOST)] = jnp.zeros((GHOST, W), jnp.float32)
-        ncls[...] = jnp.zeros((1, 32), jnp.int32)
-        nact[...] = jnp.zeros((1, 32), jnp.int32)
-
-    tables(True)
+            c.start()
+
+    @pl.when(chip == 1)
+    def _():
+        pl.semaphore_signal(ready, inc=1, device_id={"tm": core}, device_id_type=MESH)
+
+    @pl.when((chip == 0) | (chip == 3))
+    def _():
+        for c in local:
+            c.wait()
+
+    def edges_in():
+        @pl.when(takes_edge)
+        def _():
+            for c in remote:
+                c.wait_recv()
+
+        @pl.when(jnp.logical_not(takes_edge))
+        def _():
+            uw[pl.ds(land, GHOST)] = jnp.zeros((GHOST, W), jnp.float32)
+            vw[pl.ds(land, GHOST)] = jnp.zeros((GHOST, W), jnp.float32)
+            ncls[...] = jnp.zeros((1, 32), jnp.int32)
+            nact[...] = jnp.zeros((1, 32), jnp.int32)
+
+        tables(True)
+
+    @pl.when(chip == 0)
+    def _():
+        edges_in()
+        share_begins()
+
+    @pl.when(chip < 3)
+    def _():
+        share()
+
+    @pl.when(chip > 0)
+    def _():
+        edges_in()
+
     fx[0, PAD : PAD + WIN] = uw[...] * (1.0 / SF)
     fy[0, PAD : PAD + WIN] = vw[...] * (HF / SF)
-    prepare(span, GHOST, 6, cf, cg)
-
-    @pl.when(chip != 1)
+
+    @pl.when(chip == 0)
+    def _():
+        for i in range(32):
+            step(fine[i % 2], fine[(i + 1) % 2], span(31 - i), cf)
+            if i % 8 == 7:
+                rescaled(fine[0], chain[i // 8], span(0), CX, CY)
+
+    @pl.when(chip > 0)
+    def _():
+        prepare(span, GHOST, 6, cf, cg)
+
+    @pl.when(chip > 1)
     def _():
         go_on(span, GHOST, 7, 10, cg)
 
-    @pl.when((chip == 0) | (chip == 3))
-    def _():
-        n = SHARE[0]
-        base = pl.multiple_of(offset(0, 3) - SIDE, 8)
-        for q in range(8):
-            sf[q, 0 : n + 2 * SIDE] = cf[q, pl.ds(base, n + 2 * SIDE)]
-            sg[q, 0 : n + 2 * SIDE] = cg[q, pl.ds(base, n + 2 * SIDE)]
-        share((0, 3), pl.multiple_of(base + PAD, 8), sf, sg)
-
-    @pl.when(chip == 0)
-    def _():
-        for i in range(16):
-            step(fine[i % 2], fine[(i + 1) % 2], span(15 - i), cf)
-            if i == 7:
-                rescaled(fine[0], chain[2], span(0), CX, CY)
-        rescaled(fine[0], chain[3], span(0), CX, CY)
-        for k in range(2):
-            rescaled(points[k], chain[k], span(0), 1.0, 1.0)
-
     @pl.when(chip == 3)
     def _():
         go_on(span, GHOST, 11, 14, cg)
 
     @pl.when(chip > 0)
     def _():
-        lines = [(lx.at[k], ly.at[k]) for k in range(2)]
         lo, hi = (e + PAD for e in span(19))
         for i in range(4):
             k = 4 * chip - 2 + i
             lx[0, i, lo:hi] = px[k, lo:hi] * (1.0 / CX)
             ly[0, i, lo:hi] = py[k, lo:hi] * (1.0 / CY)
-        line_steps(lines, [lambda m, i=i: span(18 - i - m) for i in range(4)], cf, 8)
-        for i in range(4):
-            rescaled((lx.at[0, i], ly.at[0, i]), (lx.at[1, i], ly.at[1, i]), span(11 - i), CX, CY)
-            step((lx.at[1, i], ly.at[1, i]), (ex.at[i], ey.at[i]), span(3 - i), cg)
-        line_steps(lines, [lambda m, i=i: span(10 - i - m) for i in range(4)], cf, 8)
+        for m in range(16):
+            if m == 8:
+                for i in range(4):
+                    rescaled((lx.at[0, i], ly.at[0, i]), (lx.at[1, i], ly.at[1, i]), span(11 - i), CX, CY)
+                    step((lx.at[1, i], ly.at[1, i]), (ex.at[i], ey.at[i]), span(3 - i), cg)
+            a, b = m % 2, (m + 1) % 2
+            line_steps(
+                [((lx.at[a, i], ly.at[a, i]), (lx.at[b, i], ly.at[b, i]), span(18 - i - m)) for i in range(4)], cf
+            )
         for i in range(4):
             lo, hi = (e + PAD for e in span(3 - i))
             ex[i, lo:hi] = lx[0, i, lo:hi] * CX - ex[i, lo:hi]
             ey[i, lo:hi] = ly[0, i, lo:hi] * CY - ey[i, lo:hi]
-        for a in range(4):
+        for a in range(3):
 
             @pl.when(chip != a)
             def _(a=a):
@@ -398,7 +440,7 @@
     given = (initial_voltage, initial_recovery, block_class.reshape(1, 32), block_active.reshape(1, 32))
     given = [pltpu.with_memory_space_constraint(x, pltpu.HBM) for x in given]
     full = PAD + WIN + PAD
-    share = PAD + SHARE[1] + 2 * SIDE + PAD
+    share = PAD + SHARE + 2 * SIDE + PAD
     return pl.pallas_call(
         kernel,
         out_shape=jax.ShapeDtypeStruct((2, 2, ROWS, W), f32),
@@ -419,9 +461,9 @@
             pltpu.VMEM((2, 2, HALF, W), f32),
             *[pltpu.VMEM((2, NL, share, W), f32)] * 2,
             *[pltpu.VMEM((NL, share, W), f32)] * 4,
-            *[pltpu.VMEM((8, SHARE[1] + 2 * REACH, W), f32)] * 2,
-            *[pltpu.VMEM((8, SHARE[1] + 2 * SIDE, W), f32)] * 2,
-            pltpu.VMEM((3, 2, SHARE[1], W), f32),
+            *[pltpu.VMEM((8, SHARE + 2 * REACH, W), f32)] * 2,
+            *[pltpu.VMEM((8, SHARE + 2 * SIDE, W), f32)] * 2,
+            pltpu.VMEM((3, 2, SHARE, W), f32),
             pltpu.VMEM((2, 144, W), f32),
             pltpu.SemaphoreType.DMA((4,)),
             pltpu.SemaphoreType.DMA((4,)),
@@ -429,7 +471,7 @@
             pltpu.SemaphoreType.DMA((2,)),
             pltpu.SemaphoreType.DMA((2,)),
             pltpu.SemaphoreType.DMA((3,)),
-            pltpu.SemaphoreType.DMA((4,)),
+            pltpu.SemaphoreType.DMA((3,)),
             pltpu.SemaphoreType.REGULAR,
         ],
         compiler_params=pltpu.CompilerParams(

time: 20.3 us -> 18.3 us (0.901)
  Pallas kernels: 19.4 us -> 17.4 us
    pallas_call x1, Pallas kernels: 19.4 us -> 17.4 us  [local(): pl.pallas_call(kernel, out_shape=jax.ShapeDtypeStruct((2, 2, ROWS, W), f3...]
where the time goes in v3:
time: 18.3 us; the launch traced here: 18.2 us
  Pallas kernels  17.4 us (95%)
  local copies, waits for them, and re-layouts  0.8 us (4%)
    pallas_call x1, Pallas kernels, local(): pl.pallas_call(kernel, out_shape=jax.ShapeDtypeStruct((2, 2, ROWS, W), f3...  17.4 us
    unnamed x1, local copies, waits for them, and re-layouts  0.8 us

profile of v3, /device:TPU:71, one launch (start us, length us, event | category | flops | bytes accessed | tf_op | source)
XLA Modules:
  0.0 18.2 jit_solution(2000032713349814455)
XLA Ops:
  0.0 17.4 %shard_map.46 = f32[2,2,256,128]{3,2,1,0:T(8,128)S(1)} custom-call(f32[256,128]{1,0:T(8,128)} %u_ref.1, f32[256,128]{1,0:T(8,128)} %v_ref.1, s32[1,32]{1,0:T(1,128)} %bitcast.2, s32[1,32]{1,0:T(1,128)} %bitcast.3), custom_call_target="tpu_custom_call" | custom-call | tf_op jit(solution)/shard_map/pallas_call | solution.py:444
  17.4 0.8 %copy.6 = f32[2,2,256,128]{3,2,1,0:T(8,128)} copy(f32[2,2,256,128]{3,2,1,0:T(8,128)S(1)} %shard_map.46) | data formatting | bytes 1048576

commit v4 on v3

--- a/solution.py
+++ b/solution.py
@@ -22,6 +22,7 @@
 LOCAL = HALF + GHOST
 SHARE = 48
 SIDE = 24
+OWN = 44
 REACH = 40
 SENDS = [(a, b) for b in (1, 2, 3) for a in (0, 1, 2) if a != b]
 FIRST = 4
@@ -87,19 +88,21 @@
 ):
     t, s = lax.axis_index("tm"), lax.axis_index("space")
     chip, core = lax.div(t, 2), lax.rem(t, 2)
-    up = lax.rem(s + 17 - 2 * core, 16)
-    down = lax.rem(s + 15 + 2 * core, 16)
-    to, fro = {"space": up}, {"space": down}
-    sends_edge = s != 15 * (1 - core)
-    takes_edge = s != 15 * core
+    far = lax.div(lax.rem(s, 4), 2)
+    half = (1 - core) * (1 - far) + core * far
+    beside = s + 2 * half - 1
+    there = lax.div(lax.rem(beside + 4, 4), 2)
+    other = half * (1 - there) + (1 - half) * there
+    peer = {"tm": 2 * chip + other, "space": lax.rem(beside + 16, 16)}
+    has_peer = (beside >= 0) & (beside < 16)
     mate = {"tm": t + 1 - 2 * core}
 
     barrier = pltpu.get_barrier_semaphore()
     pl.semaphore_signal(barrier, inc=1, device_id=mate, device_id_type=MESH)
 
-    @pl.when(takes_edge)
-    def _():
-        pl.semaphore_signal(barrier, inc=1, device_id=fro, device_id_type=MESH)
+    @pl.when(has_peer)
+    def _():
+        pl.semaphore_signal(barrier, inc=1, device_id=peer, device_id_type=MESH)
 
     for a, b in ((0, 1), (2, 1), (3, 1), (1, 2), (3, 2)):
 
@@ -107,11 +110,11 @@
         def _(b=b):
             pl.semaphore_signal(barrier, inc=1, device_id={"tm": 2 * b + core}, device_id_type=MESH)
 
-    here = pl.multiple_of(80 * core, 8)
-    there = pl.multiple_of(GHOST * (1 - core), 8)
+    here = pl.multiple_of(80 * half, 8)
+    into = pl.multiple_of(GHOST * (1 - half), 8)
     local = [
-        pltpu.make_async_copy(u_ref.at[pl.ds(here, LOCAL)], uw.at[pl.ds(there, LOCAL)], lsem.at[0]),
-        pltpu.make_async_copy(v_ref.at[pl.ds(here, LOCAL)], vw.at[pl.ds(there, LOCAL)], lsem.at[1]),
+        pltpu.make_async_copy(u_ref.at[pl.ds(here, LOCAL)], uw.at[pl.ds(into, LOCAL)], lsem.at[0]),
+        pltpu.make_async_copy(v_ref.at[pl.ds(here, LOCAL)], vw.at[pl.ds(into, LOCAL)], lsem.at[1]),
         pltpu.make_async_copy(cls_ref, ocls, lsem.at[2]),
         pltpu.make_async_copy(act_ref, oact, lsem.at[3]),
     ]
@@ -123,7 +126,7 @@
             buf[k, PAD + WIN :] = jnp.zeros((PAD, W), jnp.float32)
 
     def tables(edges_here):
-        wi = lax.broadcasted_iota(jnp.int32, (32, 32), 0) + (16 * core - GHOST // BR)
+        wi = lax.broadcasted_iota(jnp.int32, (32, 32), 0) + (16 * half - GHOST // BR)
         lane = lax.broadcasted_iota(jnp.int32, (32, 32), 1)
         own = (wi >= 0) & (wi < 32)
         hot = lane == jnp.where(wi < 0, wi + 32, jnp.where(wi >= 32, wi - 32, wi))
@@ -181,6 +184,7 @@
     points = [(px.at[k], py.at[k]) for k in range(14)]
     shift = (dx, dy)
     chain = [(rx.at[k], ry.at[k]) for k in range(4)]
+
     def prepare(span, ghost, last, co, cg):
         for i in range(16):
             step(fine[i % 2], fine[(i + 1) % 2], span(ghost - 1 - i), co)
@@ -198,7 +202,7 @@
             step(points[j - 2], points[j - 1], span(ghost - 14 - j), cg, shift)
 
     def begins(a):
-        return pl.multiple_of(SHARE * (a + (2 - 2 * a) * core), 8)
+        return pl.multiple_of(SHARE * (a + (2 - 2 * a) * half), 8)
 
     def sending(a, b):
         return pltpu.make_async_remote_copy(
@@ -233,7 +237,7 @@
         def link(i):
             return tx.at[i], ty.at[i]
 
-        for tick in range(16 + 2 * NL):
+        for tick in range(16 + NL):
             if 0 <= tick < NL - 1:
                 go_on(wide, REACH, tick + 3, tick + 3, wg)
             if 0 <= tick < NL:
@@ -291,23 +295,24 @@
         tables(False)
         share_begins()
 
-    pl.semaphore_wait(barrier, 1 + sends_edge.astype(jnp.int32) + jnp.where(chip == 1, 3, jnp.where(chip == 2, 2, 0)))
-    edge = pl.multiple_of((ROWS - GHOST) * (1 - core), 8)
-    land = pl.multiple_of(LOCAL * core, 8)
+    pl.semaphore_wait(barrier, 1 + has_peer.astype(jnp.int32) + jnp.where(chip == 1, 3, jnp.where(chip == 2, 2, 0)))
+    edge = pl.multiple_of((ROWS - GHOST) * half, 8)
+    land = pl.multiple_of(LOCAL * (1 - half), 8)
+    mine = pl.multiple_of(LOCAL * half, 8)
     edges = [
+        (cls_ref, ncls),
+        (act_ref, nact),
         (u_ref.at[pl.ds(edge, GHOST)], uw.at[pl.ds(land, GHOST)]),
         (v_ref.at[pl.ds(edge, GHOST)], vw.at[pl.ds(land, GHOST)]),
-        (cls_ref, ncls),
-        (act_ref, nact),
     ]
     remote = [
         pltpu.make_async_remote_copy(
-            src_ref=a, dst_ref=b, send_sem=ssem.at[i], recv_sem=rsem.at[i], device_id=to, device_id_type=MESH
+            src_ref=a, dst_ref=b, send_sem=ssem.at[i], recv_sem=rsem.at[i], device_id=peer, device_id_type=MESH
         )
         for i, (a, b) in enumerate(edges)
     ]
 
-    @pl.when(sends_edge)
+    @pl.when(has_peer)
     def _():
         for c in remote:
             c.start()
@@ -322,19 +327,24 @@
             c.wait()
 
     def edges_in():
-        @pl.when(takes_edge)
+        @pl.when(has_peer)
         def _():
-            for c in remote:
-                c.wait_recv()
-
-        @pl.when(jnp.logical_not(takes_edge))
+            remote[0].wait_recv()
+            remote[1].wait_recv()
+
+        @pl.when(jnp.logical_not(has_peer))
         def _():
-            uw[pl.ds(land, GHOST)] = jnp.zeros((GHOST, W), jnp.float32)
-            vw[pl.ds(land, GHOST)] = jnp.zeros((GHOST, W), jnp.float32)
             ncls[...] = jnp.zeros((1, 32), jnp.int32)
             nact[...] = jnp.zeros((1, 32), jnp.int32)
+            uw[pl.ds(mine, GHOST)] = jnp.zeros((GHOST, W), jnp.float32)
+            vw[pl.ds(mine, GHOST)] = jnp.zeros((GHOST, W), jnp.float32)
 
         tables(True)
+
+        @pl.when(has_peer)
+        def _():
+            remote[2].wait_recv()
+            remote[3].wait_recv()
 
     @pl.when(chip == 0)
     def _():
@@ -361,15 +371,15 @@
 
     @pl.when(chip > 0)
     def _():
-        prepare(span, GHOST, 6, cf, cg)
+        prepare(span, OWN, 6, cf, cg)
 
     @pl.when(chip > 1)
     def _():
-        go_on(span, GHOST, 7, 10, cg)
+        go_on(span, OWN, 7, 10, cg)
 
     @pl.when(chip == 3)
     def _():
-        go_on(span, GHOST, 11, 14, cg)
+        go_on(span, OWN, 11, 14, cg)
 
     @pl.when(chip > 0)
     def _():
@@ -405,22 +415,22 @@
 
     live = mask[...] > 0.5
     mid = slice(PAD + GHOST, PAD + GHOST + HALF)
-    mine = pl.ds(pl.multiple_of(HALF * core, 8), HALF)
+    held = pl.ds(pl.multiple_of(HALF * half, 8), HALF)
     sends = []
     for i in range(2):
         k = 2 - 2 * core + i
         send[i, 0] = jnp.where(live, rx[k, mid] * SG, uw[GHOST : GHOST + HALF])
         send[i, 1] = jnp.where(live, ry[k, mid] * (SG / HG), vw[GHOST : GHOST + HALF])
         c = pltpu.make_async_remote_copy(
-            src_ref=send.at[i], dst_ref=out_ref.at[i, :, mine], send_sem=xs.at[i], recv_sem=xr.at[i],
+            src_ref=send.at[i], dst_ref=out_ref.at[i, :, held], send_sem=xs.at[i], recv_sem=xr.at[i],
             device_id=mate, device_id_type=MESH,
         )
         c.start()
         sends.append(c)
     for i in range(2):
         k = 2 * core + i
-        out_ref[i, 0, mine] = jnp.where(live, rx[k, mid] * SG, uw[GHOST : GHOST + HALF])
-        out_ref[i, 1, mine] = jnp.where(live, ry[k, mid] * (SG / HG), vw[GHOST : GHOST + HALF])
+        out_ref[i, 0, held] = jnp.where(live, rx[k, mid] * SG, uw[GHOST : GHOST + HALF])
+        out_ref[i, 1, held] = jnp.where(live, ry[k, mid] * (SG / HG), vw[GHOST : GHOST + HALF])
     for c in sends:
         c.wait()
     for a, b in SENDS:
@@ -429,7 +439,7 @@
         def _(a=a, b=b):
             sending(a, b).wait_send()
 
-    @pl.when(sends_edge)
+    @pl.when(has_peer)
     def _():
         for c in remote:
             c.wait_send()

time: 18.3 us -> 16.5 us (0.902)
  the two profiles are of different devices: /device:TPU:71 before, /device:TPU:37 now
where the time goes in v4:
time: 16.5 us; the launch traced here: 16.4 us
  Pallas kernels  15.6 us (95%)
  local copies, waits for them, and re-layouts  0.8 us (5%)
    pallas_call x1, Pallas kernels, local(): pl.pallas_call(kernel, out_shape=jax.ShapeDtypeStruct((2, 2, ROWS, W), f3...  15.6 us
    unnamed x1, local copies, waits for them, and re-layouts  0.8 us

profile of v4, /device:TPU:37, one launch (start us, length us, event | category | flops | bytes accessed | tf_op | source)
XLA Modules:
  0.0 16.4 jit_solution(5214242706747621402)
XLA Ops:
  0.0 15.6 %shard_map.46 = f32[2,2,256,128]{3,2,1,0:T(8,128)S(1)} custom-call(f32[256,128]{1,0:T(8,128)} %u_ref.1, f32[256,128]{1,0:T(8,128)} %v_ref.1, s32[1,32]{1,0:T(1,128)} %bitcast.2, s32[1,32]{1,0:T(1,128)} %bitcast.3), custom_call_target="tpu_custom_call" | custom-call | tf_op jit(solution)/shard_map/pallas_call | solution.py:454
  15.6 0.8 %copy.6 = f32[2,2,256,128]{3,2,1,0:T(8,128)} copy(f32[2,2,256,128]{3,2,1,0:T(8,128)S(1)} %shard_map.46) | data formatting | bytes 1048576
